TPU v7x, 32 devices: a whole 2x2x4 slice. The times are simulated.
32 devices in a mesh: group: 4 (over y, core), vocab: 8 (over z, x).
Axes of the slice: x: 2, y: 2, z: 4, core: 2. Of those that a mesh axis runs over, the one named last changes fastest.
Arguments:
- hidden: bfloat16 [16, 2560], P('group', 'vocab'), as said below
- dealt_slot: int32 [16], P('group'), may hold values from 0 to 15, as said below
- targets: int32 [16], P('group'), may hold values from 0 to 16383
- final_gain: float32 [2560], replicated, may hold values from 0.5 to 1.5
- vocab_head: bfloat16 [16384, 2560], P(('group', 'vocab')), as said below
- first_gain: float32 [2560], replicated, may hold values from 0.25 to 1.75
- qkv_weight: bfloat16 [2560, 3072], P(None, 'vocab'), may hold values from -0.125 to 0.125
Outputs:
- logprob: float32 [16], P('group')
- entropy: float32 [16], P('group')
- qkv_out: bfloat16 [3072, 16], P('vocab', 'group')
Inputs may be any that keep to these rules, and one draw needn't show every extreme that they name: dealt_slot is a permutation of the 16 slots; position r is owned by group r // 4, slot s belongs to group s // 4, and the positions owned by each group go exactly 1 to every group. `vocab_head`: independent rows, none zero. `hidden`: independent rows, none zero.
All inputs are finite; a program needn't handle non-finite values.
Results may differ from a plain program's by a relative error of at most 0.001.
The roundings to bfloat16 on the way count: a program that leaves them out, or rounds other values in their place, can miss the bound.
Values may be sent and summed in bfloat16 or wider, within the bound.
A program may use at most 64 MiB of HBM per device.

v0:
```python
import jax
import jax.numpy as jnp
from jax import lax
from jax.sharding import PartitionSpec as P

eps = 1e-06


def joined(array, axis, combine):
    everything = jax.tree.map(lambda part: lax.all_gather(part, axis), array)
    leading = jax.tree.map(lambda part: part[0], everything)

    def step(k, so_far):
        return combine(so_far, jax.tree.map(lambda part: part[k], everything))

    return lax.fori_loop(1, lax.axis_size(axis), step, leading)


def rms_scaled(values, gain):
    wide = values.astype(jnp.float32)
    factor = lax.rsqrt(jnp.mean(wide * wide, axis=-1, keepdims=True) + eps)
    return (wide * factor * gain).astype(jnp.bfloat16)


def merge_stats(earlier, later):
    first_top, first_total, first_weighted, first_target = earlier
    second_top, second_total, second_weighted, second_target = later
    joint_top = jnp.maximum(first_top, second_top)
    first_scale = jnp.exp(first_top - joint_top)
    second_scale = jnp.exp(second_top - joint_top)
    joint_total = first_total * first_scale + second_total * second_scale
    joint_weighted = first_scale * (
        first_weighted + first_total * (first_top - joint_top)
    ) + second_scale * (second_weighted + second_total * (second_top - joint_top))
    return (joint_top, joint_total, joint_weighted, first_target + second_target)


def local(hidden, dealt_slot, targets, final_gain, vocab_head, first_gain, qkv_weight):
    groups = lax.axis_size("group")
    shards = lax.axis_size("vocab")
    row_group = hidden.shape[0]
    col_count = hidden.shape[1]
    quota = row_group // groups
    rows_all = row_group * groups
    vocab_dev = vocab_head.shape[0]
    row_iota = jnp.arange(row_group, dtype=jnp.int32)
    dest_group = dealt_slot // row_group
    group_hits = (dest_group[:, None] == jnp.arange(groups, dtype=jnp.int32)[None, :]).astype(
        jnp.int32
    )
    earlier_hits = jnp.cumsum(group_hits, axis=0) - group_hits
    send_rank = jnp.sum(earlier_hits * group_hits, axis=1)
    position = dest_group * quota + send_rank
    packer = position[None, :] == row_iota[:, None]
    send_rows = jnp.dot(packer.astype(jnp.float32), hidden.astype(jnp.float32)).astype(jnp.bfloat16)
    send_slots = jnp.sum(jnp.where(packer, dealt_slot[None, :], 0), axis=1)
    send_targets = jnp.sum(jnp.where(packer, targets[None, :], 0), axis=1)
    arrived, arrived_slots, arrived_targets = (
        lax.all_to_all(
            send_rows.reshape(groups, quota, col_count),
            "group",
            split_axis=0,
            concat_axis=0,
            tiled=True,
        ),
        lax.all_to_all(
            send_slots.reshape(groups, quota), "group", split_axis=0, concat_axis=0, tiled=True
        ),
        lax.all_to_all(
            send_targets.reshape(groups, quota), "group", split_axis=0, concat_axis=0, tiled=True
        ),
    )
    arrived = arrived.reshape(row_group, col_count)
    local_slot = arrived_slots.reshape(row_group) % row_group
    placer = local_slot[None, :] == row_iota[:, None]
    dealt_cols = jnp.dot(placer.astype(jnp.float32), arrived.astype(jnp.float32)).astype(
        jnp.bfloat16
    )
    dealt_targets = jnp.sum(
        jnp.where(placer, arrived_targets.reshape(row_group)[None, :], 0), axis=1
    )
    dealt_rows = lax.all_gather(dealt_cols, "vocab", axis=1, tiled=True)
    normed = rms_scaled(dealt_rows, final_gain)
    offset = (lax.axis_index("group") * shards + lax.axis_index("vocab")) * vocab_dev
    vocab_iota = jnp.arange(vocab_dev, dtype=jnp.int32)
    head_wide = vocab_head.astype(jnp.float32)
    wanted_all = jnp.zeros((rows_all,), jnp.int32)
    rows_piece = lax.all_gather(normed, "group", axis=0, tiled=True)
    wanted = lax.all_gather(dealt_targets, "group", axis=0, tiled=True)
    logits = jnp.einsum("rd,vd->rv", rows_piece.astype(jnp.float32), head_wide)
    matches = (wanted - offset)[:, None] == vocab_iota[None, :]
    target_logit = jnp.sum(jnp.where(matches, logits, 0.0), axis=1)
    shard_top = jnp.max(logits, axis=1)
    shifted = logits - shard_top[:, None]
    expons = jnp.exp(shifted)
    shard_total = jnp.sum(expons, axis=1)
    shard_weighted = jnp.sum(expons * shifted, axis=1)
    shard_top, shard_total, shard_weighted, target_logit, all_targets = (
        shard_top,
        shard_total,
        shard_weighted,
        target_logit,
        lax.dynamic_update_slice_in_dim(wanted_all, wanted, jnp.int32(0), 0),
    )
    row_top, row_total, row_weighted, row_target = joined(
        (shard_top, shard_total, shard_weighted, target_logit), ("group", "vocab"), merge_stats
    )
    log_total = jnp.log(row_total)
    slot_logprob = row_target - row_top - log_total
    slot_entropy = log_total - row_weighted / row_total
    logprob = jnp.take(slot_logprob, dealt_slot, axis=0)
    entropy = jnp.take(slot_entropy, dealt_slot, axis=0)
    local_ids = all_targets - offset
    inside = (local_ids >= 0) & (local_ids < vocab_dev)
    picked_rows = jnp.take(vocab_head, jnp.clip(local_ids, 0, vocab_dev - 1), axis=0)
    partial_rows = jnp.where(inside[:, None], picked_rows, jnp.zeros_like(picked_rows))
    shared = lax.psum_scatter(
        partial_rows.astype(jnp.float32).astype(jnp.bfloat16),
        "group",
        scatter_dimension=0,
        tiled=True,
    )
    weight_wide = qkv_weight.astype(jnp.float32)
    embedded = lax.psum(shared, "vocab").astype(jnp.float32)
    first_normed = rms_scaled(embedded, first_gain)
    projected = jnp.einsum("rd,dc->cr", first_normed.astype(jnp.float32), weight_wide)
    return (logprob, entropy, projected.astype(jnp.bfloat16))


def solution(mesh):
    return jax.shard_map(
        local,
        mesh=mesh,
        in_specs=(
            P("group", "vocab"),
            P("group"),
            P("group"),
            P(),
            P(("group", "vocab"), None),
            P(),
            P(None, "vocab"),
        ),
        out_specs=(P("group"), P("group"), P("vocab", "group")),
        check_vma=False,
    )
```

profile of v0, /device:TPU:0, one launch (start us, length us, event | category | flops | bytes accessed | tf_op | source)
XLA Modules:
  0.0 167.4 jit_solution(10437662355983042251)
XLA Ops:
  7.2 0.8 compare_select_fusion.6
  8.3 0.8 select_reduce_fusion.2
  9.1 0.7 copy.23
  9.8 4.2 %all-to-all-start = ((s32[4,1,1]{2,1,0:T(1,128)}), s32[4,1,1]{2,1,0:T(1,128)S(1)}, u32[]{:S(2)}, u32[]{:S(2)}) async-start(s32[4,1,1]{2,1,0:T(1,128)} %copy.23), calls=%async_computation | async-start | bytes 4096 | tf_op jit(solution)/shard_map/all_to_all | solution.py:66
  14.0 0.8 fusion.11
  15.3 0.7 reduce.3
  16.0 0.7 reshape.149
  16.7 0.7 copy.26
  17.4 1.3 fusion.28
  20.0 3.3 %all-to-all-start.2 = ((s32[4,1,1]{2,1,0:T(1,128)}), s32[4,1,1]{2,1,0:T(1,128)S(1)}, u32[]{:S(2)}, u32[]{:S(2)}) async-start(s32[4,1,1]{2,1,0:T(1,128)} %copy.26), calls=%async_computation.2 | async-start | bytes 4096 | tf_op jit(solution)/shard_map/all_to_all | solution.py:69
  23.5 3.6 %all-to-all-done.2 = s32[4,1,1]{2,1,0:T(1,128)S(1)} async-done(((s32[4,1,1]{2,1,0:T(1,128)}), s32[4,1,1]{2,1,0:T(1,128)S(1)}, u32[]{:S(2)}, u32[]{:S(2)}) %all-to-all-start.2) | async-done | bytes 48 | tf_op jit(solution)/shard_map/all_to_all | solution.py:69
  27.1 3.2 %all-to-all-start.1 = ((bf16[4,2,160]{2,1,0:T(2,128)(2,1)}), bf16[4,2,160]{2,1,0:T(2,128)(2,1)S(1)}, u32[]{:S(2)}, u32[]{:S(2)}) async-start(bf16[4,2,160]{2,1,0:T(2,128)(2,1)} %reshape.149), calls=%async_computation.1 | async-start | bytes 8192 | tf_op jit(solution)/shard_map/all_to_all | solution.py:59
  30.9 5.4 %all-reduce.3 = s32[16]{0:T(128)S(1)} all-reduce(s32[16]{0:T(128)S(1)} %dynamic-update-slice.3), channel_id=1, replica_groups=mesh['group'=4,'vocab'=8] {'group'}, use_global_device_ids=true, to_apply=%add.3 | all-reduce | flops 16 | bytes 128
  36.9 0.7 select_select_fusion
  37.9 31.1 %all-gather.4 = bf16[8,320,4]{1,2,0:T(4,128)(2,1)S(1)} all-gather(bf16[1,320,4]{1,2,0:T(4,128)(2,1)S(1)} %fusion.12), channel_id=1, replica_groups=mesh['group'=4,'vocab'=8] {'vocab'}, dimensions={0}, use_global_device_ids=true | all-gather | bytes 23040 | tf_op jit(solution)/shard_map/all_gather | solution.py:82
  69.2 0.8 fusion.17
  70.0 5.3 %all-gather.5 = bf16[4,4,2560]{2,1,0:T(4,128)(2,1)S(1)} all-gather(bf16[1,4,2560]{2,1,0:T(4,128)(2,1)S(1)} %fusion.17), channel_id=1, replica_groups=mesh['group'=4,'vocab'=8] {'group'}, dimensions={0}, use_global_device_ids=true | all-gather | bytes 102400 | tf_op jit(solution)/shard_map/all_gather | solution.py:88
  75.3 0.9 fusion.29
  77.3 38.9 %all-reduce.6 = (f32[512]{0:T(512)S(1)}, f32[512]{0:T(512)S(1)}, f32[512]{0:T(512)S(1)}, f32[512]{0:T(512)S(1)}) all-reduce(f32[512]{0:T(512)S(1)} %dynamic-update-slice, f32[512]{0:T(512)S(1)} %dynamic-update-slice.1, f32[512]{0:T(512)S(1)} %dynamic-update-slice.2, ...), channel_id=2, replica_groups=mesh['group'=4,'vocab'=8] {'group','vocab'}, use_global_device_ids=true, to_apply=%add | all-reduce | flops 2048 | bytes 16384
  116.5 2.7 %while.21 = (s32[]{:T(128)}, f32[16]{0:T(128)S(1)}, f32[16]{0:T(128)S(1)}, f32[16]{0:T(128)S(1)}, f32[16]{0:T(128)S(1)}, /*index=5*/f32[32,16]{1,0:T(8,128)S(1)}...) while((s32[]{:T(128)}, f32[16]{0:T(128)S(1)}, ...), condition=%wide.region_11.12_spmd, body=%wide.region_10.11_spmd.sunk | while | flops 261 | bytes 1383 | solution.py:16
  119.2 0.6 gather_fusion.2
  121.0 0.8 constant_dynamic-slice_fusion.4
  121.8 36.1 %psum.7 = bf16[4,2560]{1,0:T(4,128)(2,1)S(1)} all-reduce(bf16[4,2560]{1,0:T(4,128)(2,1)S(1)} %constant_dynamic-slice_fusion.4), channel_id=1, replica_groups=mesh['group'=4,'vocab'=8] {'vocab'}, use_global_device_ids=true, to_apply=%region_13.15 | all-reduce | flops 10240 | bytes 40960 | tf_op jit(solution)/shard_map/psum | solution.py:124
  158.0 2.5 %fusion.10 = bf16[384,4]{0,1:T(4,128)(2,1)} fusion(bf16[2560,384]{1,0:T(8,128)(2,1)} %param.17, bf16[4,2560]{1,0:T(4,128)(2,1)S(1)} %psum.7, f32[2560]{0:T(1024)S(1)} %copy-done.1, f32[4]{0:T(128)S(1)} %add_rsqrt_fusion), kind=kOutput, calls=%fused_computation.21 | convolution fusion | flops 7906816 | bytes 1999888 | tf_op jit(solution)/shard_map/rd,dc->cr/dot_general | solution.py:126
  (149 shorter events, 7.2 us)
Async XLA Ops:
  7.2 29.1 %copy-start = (bf16[512,2560]{1,0:T(8,128)(2,1)S(1)}, bf16[512,2560]{1,0:T(8,128)(2,1)}, u32[]{:S(2)}) copy-start(bf16[512,2560]{1,0:T(8,128)(2,1)} %param.15) | copy-start | bytes 7864324
  9.8 10.2 %all-to-all-start = ((s32[4,1,1]{2,1,0:T(1,128)}), s32[4,1,1]{2,1,0:T(1,128)S(1)}, u32[]{:S(2)}, u32[]{:S(2)}) async-start(s32[4,1,1]{2,1,0:T(1,128)} %copy.23), calls=%async_computation | async-start | bytes 4096 | tf_op jit(solution)/shard_map/all_to_all | solution.py:66
  20.0 7.1 %all-to-all-start.2 = ((s32[4,1,1]{2,1,0:T(1,128)}), s32[4,1,1]{2,1,0:T(1,128)S(1)}, u32[]{:S(2)}, u32[]{:S(2)}) async-start(s32[4,1,1]{2,1,0:T(1,128)} %copy.26), calls=%async_computation.2 | async-start | bytes 4096 | tf_op jit(solution)/shard_map/all_to_all | solution.py:69
  27.1 10.6 %all-to-all-start.1 = ((bf16[4,2,160]{2,1,0:T(2,128)(2,1)}), bf16[4,2,160]{2,1,0:T(2,128)(2,1)S(1)}, u32[]{:S(2)}, u32[]{:S(2)}) async-start(bf16[4,2,160]{2,1,0:T(2,128)(2,1)} %reshape.149), calls=%async_computation.1 | async-start | bytes 8192 | tf_op jit(solution)/shard_map/all_to_all | solution.py:59
  30.3 90.7 %all-reduce.9.cloned.1.call-start = ((), (), s32[]{:S(2)}) async-start(), calls=%async_computation.3 | async-start | bytes 163840
  36.9 83.6 %copy-start.2 = (s32[4]{0:T(128)S(1)}, s32[4]{0:T(128)}, u32[]{:S(2)}) copy-start(s32[4]{0:T(128)} %param.12) | copy-start | bytes 52
  36.9 121.1 %copy-start.1 = (f32[2560]{0:T(1024)S(1)}, f32[2560]{0:T(1024)}, u32[]{:S(2)}) copy-start(f32[2560]{0:T(1024)} %param.16) | copy-start | bytes 30724
Sparse Core Ops, SparseCore 0:
  37.8 30.6 all-reduce.8
where the time goes:
time: 168 us; the launch traced here: 167 us
  blocking collectives  117 us (70%)
  between operations  15.5 us (9%)
  starting transfers between devices  10.8 us (6%)
  local copies, waits for them, and re-layouts  8.28 us (5%)
  other arithmetic  7.31 us (4%)
  matrix products  4.37 us (3%)
  waiting for transfers between devices  3.6 us (2%)
    unnamed x2, blocking collectives  44.2 us
    psum x1, blocking collectives, local(): embedded = lax.psum(shared, 'vocab').astype(jnp.float32)  36.1 us
    all_gather x1, blocking collectives, local(): dealt_rows = lax.all_gather(dealt_cols, 'vocab', axis=1, tiled=True)  31.1 us
    all_gather x1, blocking collectives, local(): rows_piece = lax.all_gather(normed, 'group', axis=0, tiled=True)  5.29 us
    all_to_all x1, starting transfers between devices, local(): lax.all_to_all(send_slots.reshape(groups, quota), 'group', split_axis=0,...  4.24 us
    unnamed x21, local copies, waits for them, and re-layouts  4.04 us
    all_to_all x1, waiting for transfers between devices, local(): lax.all_to_all(send_targets.reshape(groups, quota), 'group', split_axis=0...  3.58 us
  transfers between devices with their start and end apart: 4, of which 1 were waited for; matrix products, arithmetic and copies ran while one was open for 8% of the time, Pallas kernels for 0%

commit v1 on v0

--- a/solution.py
+++ b/solution.py
@@ -121,7 +121,7 @@
         tiled=True,
     )
     weight_wide = qkv_weight.astype(jnp.float32)
-    embedded = lax.psum(shared, "vocab").astype(jnp.float32)
+    embedded = jnp.sum(lax.all_gather(shared, "vocab"), axis=0).astype(jnp.float32)
     first_normed = rms_scaled(embedded, first_gain)
     projected = jnp.einsum("rd,dc->cr", first_normed.astype(jnp.float32), weight_wide)
     return (logprob, entropy, projected.astype(jnp.bfloat16))

time: 168 us -> 163 us (0.970)
  blocking collectives: 117 us -> 111 us
    psum x1 -> x0, blocking collectives: 36.1 us -> none  [local(): embedded = lax.psum(shared, 'vocab').astype(jnp.float32)]
    all_gather x0 -> x1, blocking collectives: none -> 30.7 us  [local(): lax.all_gather(shared, 'vocab')]
  transfers between devices with their start and end apart: 4 -> 4, of which waited for: 1 -> 1; matrix products, arithmetic and copies ran while one was open for 8% -> 9% of each run, Pallas kernels for 0% -> 0%
where the time goes in v1:
time: 163 us; the launch traced here: 162 us
  blocking collectives  111 us (68%)
  between operations  15.5 us (10%)
  starting transfers between devices  10.8 us (7%)
  local copies, waits for them, and re-layouts  8.27 us (5%)
  other arithmetic  7.33 us (4%)
  matrix products  4.37 us (3%)
  waiting for transfers between devices  3.6 us (2%)
    unnamed x2, blocking collectives  44.2 us
    all_gather x1, blocking collectives, local(): dealt_rows = lax.all_gather(dealt_cols, 'vocab', axis=1, tiled=True)  31.1 us
    all_gather x1, blocking collectives, local(): lax.all_gather(shared, 'vocab')  30.7 us
    all_gather x1, blocking collectives, local(): rows_piece = lax.all_gather(normed, 'group', axis=0, tiled=True)  5.29 us
    all_to_all x1, starting transfers between devices, local(): lax.all_to_all(send_slots.reshape(groups, quota), 'group', split_axis=0,...  4.24 us
    unnamed x21, local copies, waits for them, and re-layouts  4.04 us
    all_to_all x1, waiting for transfers between devices, local(): lax.all_to_all(send_targets.reshape(groups, quota), 'group', split_axis=0...  3.58 us
    all_to_all x1, starting transfers between devices, local(): lax.all_to_all(send_targets.reshape(groups, quota), 'group', split_axis=0...  3.3 us
  transfers between devices with their start and end apart: 4, of which 1 were waited for; matrix products, arithmetic and copies ran while one was open for 9% of the time, Pallas kernels for 0%

profile of v1, /device:TPU:0, one launch (start us, length us, event | category | flops | bytes accessed | tf_op | source)
XLA Modules:
  0.0 162.0 jit_solution(15680930993682646409)
XLA Ops:
  7.2 0.8 compare_select_fusion.6
  8.3 0.8 select_reduce_fusion.2
  9.1 0.7 copy.23
  9.8 4.2 %all-to-all-start = ((s32[4,1,1]{2,1,0:T(1,128)}), s32[4,1,1]{2,1,0:T(1,128)S(1)}, u32[]{:S(2)}, u32[]{:S(2)}) async-start(s32[4,1,1]{2,1,0:T(1,128)} %copy.23), calls=%async_computation | async-start | bytes 4096 | tf_op jit(solution)/shard_map/all_to_all | solution.py:66
  14.0 0.7 copy.26
  14.7 0.8 fusion.11
  16.0 0.7 reduce.5
  16.7 0.7 reshape.153
  17.4 1.3 fusion.28
  20.0 3.3 %all-to-all-start.2 = ((s32[4,1,1]{2,1,0:T(1,128)}), s32[4,1,1]{2,1,0:T(1,128)S(1)}, u32[]{:S(2)}, u32[]{:S(2)}) async-start(s32[4,1,1]{2,1,0:T(1,128)} %copy.26), calls=%async_computation.2 | async-start | bytes 4096 | tf_op jit(solution)/shard_map/all_to_all | solution.py:69
  23.5 3.6 %all-to-all-done.2 = s32[4,1,1]{2,1,0:T(1,128)S(1)} async-done(((s32[4,1,1]{2,1,0:T(1,128)}), s32[4,1,1]{2,1,0:T(1,128)S(1)}, u32[]{:S(2)}, u32[]{:S(2)}) %all-to-all-start.2) | async-done | bytes 48 | tf_op jit(solution)/shard_map/all_to_all | solution.py:69
  27.1 3.2 %all-to-all-start.1 = ((bf16[4,2,160]{2,1,0:T(2,128)(2,1)}), bf16[4,2,160]{2,1,0:T(2,128)(2,1)S(1)}, u32[]{:S(2)}, u32[]{:S(2)}) async-start(bf16[4,2,160]{2,1,0:T(2,128)(2,1)} %reshape.153), calls=%async_computation.1 | async-start | bytes 8192 | tf_op jit(solution)/shard_map/all_to_all | solution.py:59
  30.9 5.4 %all-reduce.3 = s32[16]{0:T(128)S(1)} all-reduce(s32[16]{0:T(128)S(1)} %dynamic-update-slice.3), channel_id=1, replica_groups=mesh['group'=4,'vocab'=8] {'group'}, use_global_device_ids=true, to_apply=%add.3 | all-reduce | flops 16 | bytes 128
  36.9 0.7 select_select_fusion
  37.8 31.1 %all-gather.5 = bf16[8,320,4]{1,2,0:T(4,128)(2,1)S(1)} all-gather(bf16[1,320,4]{1,2,0:T(4,128)(2,1)S(1)} %fusion.12), channel_id=1, replica_groups=mesh['group'=4,'vocab'=8] {'vocab'}, dimensions={0}, use_global_device_ids=true | all-gather | bytes 23040 | tf_op jit(solution)/shard_map/all_gather | solution.py:82
  69.1 0.8 fusion.17
  69.9 5.3 %all-gather.6 = bf16[4,4,2560]{2,1,0:T(4,128)(2,1)S(1)} all-gather(bf16[1,4,2560]{2,1,0:T(4,128)(2,1)S(1)} %fusion.17), channel_id=1, replica_groups=mesh['group'=4,'vocab'=8] {'group'}, dimensions={0}, use_global_device_ids=true | all-gather | bytes 102400 | tf_op jit(solution)/shard_map/all_gather | solution.py:88
  75.3 0.9 fusion.29
  77.3 38.9 %all-reduce.6 = (f32[512]{0:T(512)S(1)}, f32[512]{0:T(512)S(1)}, f32[512]{0:T(512)S(1)}, f32[512]{0:T(512)S(1)}) all-reduce(f32[512]{0:T(512)S(1)} %dynamic-update-slice, f32[512]{0:T(512)S(1)} %dynamic-update-slice.1, f32[512]{0:T(512)S(1)} %dynamic-update-slice.2, ...), channel_id=2, replica_groups=mesh['group'=4,'vocab'=8] {'group','vocab'}, use_global_device_ids=true, to_apply=%add | all-reduce | flops 2048 | bytes 16384
  116.5 2.6 %while.21 = (s32[]{:T(128)}, f32[16]{0:T(128)S(1)}, f32[16]{0:T(128)S(1)}, f32[16]{0:T(128)S(1)}, f32[16]{0:T(128)S(1)}, /*index=5*/f32[32,16]{1,0:T(8,128)S(1)}...) while((s32[]{:T(128)}, f32[16]{0:T(128)S(1)}, ...), condition=%wide.region_11.12_spmd, body=%wide.region_10.11_spmd.sunk | while | flops 261 | bytes 1375 | solution.py:16
  119.1 0.6 gather_fusion.2
  120.9 0.8 dynamic-slice_bitcast_fusion
  121.7 30.7 %all-gather.7 = bf16[8,4,2560]{2,1,0:T(4,128)(2,1)S(1)} all-gather(bf16[1,4,2560]{2,1,0:T(4,128)(2,1)S(1)} %dynamic-slice_bitcast_fusion), channel_id=6, replica_groups=mesh['group'=4,'vocab'=8] {'vocab'}, dimensions={0}, use_global_device_ids=true | all-gather | bytes 184320 | tf_op jit(solution)/shard_map/all_gather | solution.py:124
  152.6 2.5 %fusion.10 = bf16[384,4]{0,1:T(4,128)(2,1)} fusion(bf16[2560,384]{1,0:T(8,128)(2,1)} %param.17, bf16[4,2560]{1,0:T(4,128)(2,1)S(1)} %reduce_sum.101, f32[2560]{0:T(1024)S(1)} %copy-done.1, f32[4]{0:T(128)S(1)} %add_rsqrt_fusion), kind=kOutput, calls=%fused_computation.21 | convolution fusion | flops 7906816 | bytes 1999888 | tf_op jit(solution)/shard_map/rd,dc->cr/dot_general | solution.py:126
  (150 shorter events, 7.2 us)
Async XLA Ops:
  7.2 29.1 %copy-start = (bf16[512,2560]{1,0:T(8,128)(2,1)S(1)}, bf16[512,2560]{1,0:T(8,128)(2,1)}, u32[]{:S(2)}) copy-start(bf16[512,2560]{1,0:T(8,128)(2,1)} %param.15) | copy-start | bytes 7864324
  9.8 10.2 %all-to-all-start = ((s32[4,1,1]{2,1,0:T(1,128)}), s32[4,1,1]{2,1,0:T(1,128)S(1)}, u32[]{:S(2)}, u32[]{:S(2)}) async-start(s32[4,1,1]{2,1,0:T(1,128)} %copy.23), calls=%async_computation | async-start | bytes 4096 | tf_op jit(solution)/shard_map/all_to_all | solution.py:66
  20.0 7.1 %all-to-all-start.2 = ((s32[4,1,1]{2,1,0:T(1,128)}), s32[4,1,1]{2,1,0:T(1,128)S(1)}, u32[]{:S(2)}, u32[]{:S(2)}) async-start(s32[4,1,1]{2,1,0:T(1,128)} %copy.26), calls=%async_computation.2 | async-start | bytes 4096 | tf_op jit(solution)/shard_map/all_to_all | solution.py:69
  27.1 10.6 %all-to-all-start.1 = ((bf16[4,2,160]{2,1,0:T(2,128)(2,1)}), bf16[4,2,160]{2,1,0:T(2,128)(2,1)S(1)}, u32[]{:S(2)}, u32[]{:S(2)}) async-start(bf16[4,2,160]{2,1,0:T(2,128)(2,1)} %reshape.153), calls=%async_computation.1 | async-start | bytes 8192 | tf_op jit(solution)/shard_map/all_to_all | solution.py:59
  30.3 90.6 %all-reduce.9.cloned.1.call-start = ((), (), s32[]{:S(2)}) async-start(), calls=%async_computation.3 | async-start | bytes 163840
  36.9 83.5 %copy-start.2 = (s32[4]{0:T(128)S(1)}, s32[4]{0:T(128)}, u32[]{:S(2)}) copy-start(s32[4]{0:T(128)} %param.12) | copy-start | bytes 52
  68.9 83.7 %copy-start.1 = (f32[2560]{0:T(1024)S(1)}, f32[2560]{0:T(1024)}, u32[]{:S(2)}) copy-start(f32[2560]{0:T(1024)} %param.16) | copy-start | bytes 30724
Sparse Core Ops, SparseCore 0:
  37.7 30.6 all-reduce.8
